TPU v7x, 32 devices: a whole 2x2x4 slice. The times are simulated.
32 devices in a mesh: blocks: 2 (over y), space: 4 (over z), tm: 2 (over x), span: 2 (over core).
Axes of the slice: x: 2, y: 2, z: 4, core: 2. Of those that a mesh axis runs over, the one named last changes fastest.
Arguments:
- snapshots: float32 [320, 64, 512], P(('blocks', 'tm'), 'space', 'span'), parts along dimension 0, may hold values from -6 to 6
- lagrange_weights: float32 [512, 6], P(('blocks', 'tm')), parts along dimension 0, may hold values from -3 to 3
- source_start: int32 [512], P(('blocks', 'tm')), parts along dimension 0, may hold values from 0 to 156
- band_len: int32 [512], P(('blocks', 'tm')), parts along dimension 0, may hold values from 4 to 6
- band_list: int32 [8], replicated, may hold values from 0 to 15, as said below
- row_metric: float32 [64], P('space'), may hold values from 0.5 to 2
Outputs:
- spectra: float32 [256, 2, 64, 512], P(('blocks', 'space', 'tm'), None, None, 'span'), parts along dimension 0
There are 2 independent parts, one for each index of `blocks`. A program takes and returns all parts, laid end to end along the dimension named above; an argument that names none is the same for every part. Nothing has to cross between parts.
Inputs may be any that keep to these rules, and one draw needn't show every extreme that they name: `band_list`: 8 distinct band numbers.
All inputs are finite; a program needn't handle non-finite values.
Results may differ from a plain program's by a relative error of at most 0.0001.
Values sent between devices are 32-bit elements; how exact they have to be, the bound alone decides.
A program may use at most 64 MiB of HBM per device.

v0:
```python
import math

import jax
import jax.numpy as jnp
from jax import lax
from jax.sharding import PartitionSpec as P

HALO = 16
NT = 256
BW = 8
NL = 8


def extended(cells, sides, width, closed):
    for axis, dim in sides:
        count = lax.axis_size(axis)
        ends = count if closed else count - 1
        head = lax.slice_in_dim(cells, 0, width, axis=dim)
        tail = lax.slice_in_dim(cells, cells.shape[dim] - width, cells.shape[dim], axis=dim)
        cells = jnp.concatenate(
            [
                lax.ppermute(tail, axis, [(i, (i + 1) % count) for i in range(ends)]),
                cells,
                lax.ppermute(head, axis, [((i + 1) % count, i) for i in range(ends)]),
            ],
            axis=dim,
        )
    return cells


def dft_rows(band_list, row_ids, first_sample, count):
    listed_idx = row_ids // 2
    is_imag = row_ids % 2
    band_pos = listed_idx // BW
    matches = band_pos[:, None] == jnp.arange(band_list.shape[0])[None, :]
    band_of = jnp.sum(jnp.where(matches, band_list[None, :], 0), axis=1)
    frequency = band_of * BW + listed_idx % BW
    sample_ids = first_sample + jnp.arange(count)
    phase_idx = frequency[:, None] * sample_ids[None, :] % NT
    angles = 2.0 * math.pi / NT * phase_idx.astype(jnp.float32)
    window = 0.5 - 0.5 * jnp.cos(2.0 * math.pi / NT * sample_ids.astype(jnp.float32))
    weighting = window / math.sqrt(NT)
    waves = jnp.where(is_imag[:, None] == 0, jnp.cos(angles), -jnp.sin(angles))
    return waves * weighting[None, :]


def spatial_gradients(fields, metric):
    row_padded = extended(fields, (("space", 1),), 1, False)
    along_rows = 0.5 * metric[None, :, None] * (row_padded[:, 2:, :] - row_padded[:, :-2, :])
    span_padded = extended(fields, (("span", 2),), 1, True)
    along_span = 0.5 * (span_padded[:, :, 2:] - span_padded[:, :, :-2])
    return jnp.stack((along_rows, along_span), axis=1)


def shards(snapshots, lagrange_weights, source_start, band_len, band_list, row_metric):
    tm_index = lax.axis_index("tm")
    steps_dev, rows_dev, span_cells = snapshots.shape
    samples = source_start.shape[0]
    reach = extended(snapshots, (("tm", 0),), HALO, False)
    reach_len = steps_dev + 2 * HALO
    anchor = tm_index * steps_dev - HALO
    slot_ids = jnp.arange(6)
    columns = source_start[:, None] + slot_ids[None, :] - anchor
    active = slot_ids[None, :] < band_len[:, None]
    selected = (columns[:, :, None] == jnp.arange(reach_len)[None, None, :]) & active[:, :, None]
    interp_matrix = jnp.sum(
        jnp.where(selected, lagrange_weights[:, :, None], jnp.float32(0.0)), axis=1
    )
    flat_reach = reach.reshape(reach_len, rows_dev * span_cells)
    total_rows = 2 * NL * BW
    positions = jnp.arange(total_rows)
    coeffs = dft_rows(band_list, positions, tm_index * samples, samples)
    interpolated = jnp.dot(interp_matrix, flat_reach, precision=lax.Precision.HIGHEST)
    gradients = spatial_gradients(interpolated.reshape(samples, rows_dev, span_cells), row_metric)
    partial_value = jnp.dot(
        coeffs,
        gradients.reshape(samples, 2 * rows_dev * span_cells),
        precision=lax.Precision.HIGHEST,
    )
    shaped = partial_value.reshape(total_rows, 2, rows_dev, span_cells)
    arrived = lax.all_to_all(shaped, "space", split_axis=0, concat_axis=2, tiled=True)
    return lax.psum_scatter(arrived, "tm", scatter_dimension=0, tiled=True)


def solution(mesh):
    placed = (
        P(("blocks", "tm"), "space", "span"),
        P(("blocks", "tm"), None),
        P(("blocks", "tm")),
        P(("blocks", "tm")),
        P(),
        P("space"),
    )
    return jax.shard_map(
        shards,
        mesh=mesh,
        in_specs=placed,
        out_specs=P(("blocks", "space", "tm"), None, None, "span"),
        check_vma=False,
    )
```

profile of v0, /device:TPU:0, one launch (start us, length us, event | category | flops | bytes accessed | tf_op | source)
XLA Modules:
  0.0 219.2 jit_solution(1582973083765594026)
XLA Ops:
  6.5 0.0 reduce-scatter.2.cloned.1.call-start
  6.5 1.1 fusion.42
  7.6 4.9 %collective-permute-start = (f32[16,16,256]{2,1,0:T(8,128)S(1)}, f32[16,16,256]{2,1,0:T(8,128)S(1)}, u32[]{:S(2)}, u32[]{:S(2)}) collective-permute-start(f32[16,16,256]{2,1,0:T(8,128)S(1)} %get-tuple-element.11), channel_id=1, source_target_pairs={{0,2},{1,3},{4,6},{5,7},{8,10},{9,11},{12,14},{13,15},{16,18},{17,... | collective-permute-start | bytes 786440 | tf_op jit(solution)/shard_map/ppermute | solution.py:22
  12.5 1.3 collective-permute-start.1
  13.8 0.7 iota_compare_fusion.1
  14.5 1.2 broadcast_multiply_fusion
  15.7 0.7 add_subtract_fusion
  16.4 0.7 select_reduce_fusion.1
  17.1 0.8 select_reduce_fusion
  17.9 0.6 subtract_multiply_fusion
  18.5 0.6 fusion.34
  19.1 0.0 collective-permute-done
  19.1 3.0 %collective-permute-done.1 = f32[16,16,256]{2,1,0:T(8,128)S(1)} collective-permute-done((f32[16,16,256]{2,1,0:T(8,128)S(1)}, f32[16,16,256]{2,1,0:T(8,128)S(1)}, u32[]{:S(2)}, u32[]{:S(2)}) %collective-permute-start.1) | collective-permute-done | bytes 262176 | tf_op jit(solution)/shard_map/ppermute | solution.py:24
  22.1 1.5 pad_maximum_fusion.5
  23.6 2.8 %fusion.8 = f32[128,16,256]{2,0,1:T(8,128)S(1)} fusion(f32[128,112]{0,1:T(8,128)S(1)} %select_reduce_fusion, f32[14,8,16,256]{3,2,1,0:T(8,128)S(1)} %bitcast.36), kind=kOutput, calls=%fused_computation.13 | convolution fusion | flops 704643072 | bytes 3989504 | tf_op jit(solution)/shard_map/dot_general | solution.py:73
  26.4 0.7 fusion.40
  27.1 1.3 collective-permute-start.2
  28.4 4.7 %collective-permute-start.3 = (f32[128,1,256]{2,0,1:T(8,128)S(1)}, f32[128,1,256]{2,0,1:T(8,128)S(1)}, u32[]{:S(2)}, u32[]{:S(2)}) collective-permute-start(f32[128,1,256]{2,0,1:T(8,128)S(1)} %get-tuple-element.8), channel_id=1, source_target_pairs={{0,4},{4,8},{8,12},{1,5},{5,9},{9,13},{2,6},{6,10},{10,14},{3,7},{... | collective-permute-start | bytes 393224 | tf_op jit(solution)/shard_map/ppermute | solution.py:22
  33.1 1.3 fusion.41
  34.4 1.6 copy.23
  36.0 0.0 collective-permute-start.4
  36.0 0.9 copy.25
  37.0 0.5 collective-permute-start.5
  37.5 0.6 fusion.35
  38.0 0.0 collective-permute-done.4
  38.1 0.0 copy-start.2
  38.1 0.4 copy.24
  38.4 0.2 collective-permute-done.5
  38.6 2.0 copy.26
  40.7 0.0 collective-permute-done.2
  40.7 0.0 collective-permute-done.3
  40.7 0.0 copy-done.2
  40.7 2.8 %fusion.7 = (f32[128,1,16,256]{3,0,2,1:T(8,128)S(1)}, f32[128,1,16,256]{3,0,2,1:T(8,128)S(1)}) fusion(f32[128,16,256]{2,0,1:T(8,128)S(1)} %fusion.8, f32[128,1,256]{2,0,1:T(8,128)S(1)} %collective-permute-done.3, f32[128,1,256]{2,0,1:T(8,128)S(1)} %collective-permute-done.2, f32[16]{0:T(128)S(1)} %copy-done.2, f32[128,16,1]{2,0,1:T(8,128)} %copy.26, ...), kind=kLoop, calls=%fused_computation.11 | loop fusion | flops 4194304 | bytes 6570048 | tf_op jit(solution)/shard_map/stack | solution.py:52
  43.4 2.2 %pad_maximum_fusion = f32[128,2,16,256]{3,0,2,1:T(8,128)} fusion(f32[128,1,16,256]{3,0,2,1:T(8,128)S(1)} %get-tuple-element.6, f32[128,1,16,256]{3,0,2,1:T(8,128)S(1)} %get-tuple-element.5), kind=kLoop, calls=%fused_computation | loop fusion | flops 1048576 | bytes 8388608 | tf_op jit(solution)/shard_map/stack | solution.py:52
  45.7 0.0 copy-start
  45.7 0.0 copy-start.1
  45.7 0.0 copy-start.3
  45.7 5.4 %copy.27 = f32[128,2,16,256]{0,3,2,1:T(8,128)} copy(f32[128,2,16,256]{3,0,2,1:T(8,128)} %pad_maximum_fusion) | data formatting | bytes 8388608 | tf_op jit(solution)/shard_map/stack | solution.py:52
  51.1 0.0 copy-done
  51.1 0.0 copy-done.1
  51.1 0.0 copy-done.3
  51.1 0.0 copy-done.4
  51.1 6.2 %fusion = f32[128,2,16,256]{3,0,2,1:T(8,128)S(1)} fusion(f32[128,2,16,256]{0,3,2,1:T(8,128)} %copy.27, f32[128]{0:T(128)S(1)} %copy-done.3, s32[128]{0:T(128)S(1)} %copy-done.1, s32[128]{0:T(128)S(1)} %copy-done, pred[128]{0:T(512)(128)(4,1)S(1)} %copy-done.4), kind=kOutput, calls=%fused_computation.1 | convolution fusion | flops 1610891264 | bytes 8390272 | tf_op jit(solution)/shard_map/dot_general | solution.py:75
  57.3 2.4 %copy.28 = f32[128,2,16,256]{3,2,1,0:T(8,128)S(1)} copy(f32[128,2,16,256]{3,0,2,1:T(8,128)S(1)} %fusion) | data formatting | bytes 8388608 | tf_op jit(solution)/shard_map/dot_general | solution.py:75
  59.7 97.3 %all_to_all.18 = f32[128,2,16,256]{3,2,1,0:T(8,128)S(1)} all-to-all(f32[128,2,16,256]{3,2,1,0:T(8,128)S(1)} %copy.28), channel_id=1, replica_groups=mesh['blocks'=2,'space'=4,'tm'=2,'span'=2] {'space'}, dimensions={0} | all-to-all | bytes 8388608 | tf_op jit(solution)/shard_map/all_to_all | solution.py:81
  157.0 2.6 %copy.29 = f32[32,2,4,16,256]{4,3,2,1,0:T(8,128)} copy(f32[32,2,4,16,256]{4,3,1,0,2:T(8,128)S(1)} %bitcast.35) | data formatting | bytes 8388608 | tf_op jit(solution)/shard_map/all_to_all | solution.py:81
  159.7 0.0 reduce-scatter.2.cloned.1.call-update
  159.7 52.6 %reduce-scatter.2.cloned.1.call-done = f32[16,2,64,256]{3,2,1,0:T(8,128)} async-done(((f32[32,2,64,256]{3,2,1,0:T(8,128)}), f32[16,2,64,256]{3,2,1,0:T(8,128)}) %reduce-scatter.2.cloned.1.call-update) | async-done | bytes 2097168 | tf_op jit(solution)/shard_map/reduce_scatter | solution.py:82
  (2 shorter events, 0.0 us)
Async XLA Ops:
  6.5 205.8 %reduce-scatter.2.cloned.1.call-start = ((), (), s32[]{:S(2)}) async-start(), calls=%async_computation.2 | async-start | bytes 6291456 | tf_op jit(solution)/shard_map/reduce_scatter | solution.py:82
  7.6 11.5 %collective-permute-start = (f32[16,16,256]{2,1,0:T(8,128)S(1)}, f32[16,16,256]{2,1,0:T(8,128)S(1)}, u32[]{:S(2)}, u32[]{:S(2)}) collective-permute-start(f32[16,16,256]{2,1,0:T(8,128)S(1)} %get-tuple-element.11), channel_id=1, source_target_pairs={{0,2},{1,3},{4,6},{5,7},{8,10},{9,11},{12,14},{13,15},{16,18},{17,... | collective-permute-start | bytes 786440 | tf_op jit(solution)/shard_map/ppermute | solution.py:22
  12.5 9.7 %collective-permute-start.1 = (f32[16,16,256]{2,1,0:T(8,128)S(1)}, f32[16,16,256]{2,1,0:T(8,128)S(1)}, u32[]{:S(2)}, u32[]{:S(2)}) collective-permute-start(f32[16,16,256]{2,1,0:T(8,128)S(1)} %get-tuple-element.12), channel_id=1, source_target_pairs={{2,0},{3,1},{6,4},{7,5},{10,8},{11,9},{14,12},{15,13},{18,16},{19,... | collective-permute-start | bytes 786440 | tf_op jit(solution)/shard_map/ppermute | solution.py:24
  27.1 13.6 %collective-permute-start.2 = (f32[128,1,256]{2,0,1:T(8,128)}, f32[128,1,256]{2,0,1:T(8,128)S(1)}, u32[]{:S(2)}, u32[]{:S(2)}) collective-permute-start(f32[128,1,256]{2,0,1:T(8,128)} %get-tuple-element.7), channel_id=1, source_target_pairs={{4,0},{8,4},{12,8},{5,1},{9,5},{13,9},{6,2},{10,6},{14,10},{7,3},{... | collective-permute-start | bytes 393224 | tf_op jit(solution)/shard_map/ppermute | solution.py:24
  28.4 12.3 %collective-permute-start.3 = (f32[128,1,256]{2,0,1:T(8,128)S(1)}, f32[128,1,256]{2,0,1:T(8,128)S(1)}, u32[]{:S(2)}, u32[]{:S(2)}) collective-permute-start(f32[128,1,256]{2,0,1:T(8,128)S(1)} %get-tuple-element.8), channel_id=1, source_target_pairs={{0,4},{4,8},{8,12},{1,5},{5,9},{9,13},{2,6},{6,10},{10,14},{3,7},{... | collective-permute-start | bytes 393224 | tf_op jit(solution)/shard_map/ppermute | solution.py:22
  36.0 2.1 collective-permute-start.4
  37.0 1.7 collective-permute-start.5
  38.1 2.6 %copy-start.2 = (f32[16]{0:T(128)S(1)}, f32[16]{0:T(128)}, u32[]{:S(2)}) copy-start(f32[16]{0:T(128)} %broadcast_multiply_fusion) | copy-start | bytes 196
  45.7 5.4 %copy-start = (s32[128]{0:T(128)S(1)}, s32[128]{0:T(128)}, u32[]{:S(2)}) copy-start(s32[128]{0:T(128)} %get-tuple-element.13) | copy-start | bytes 1540
  45.7 5.4 %copy-start.1 = (s32[128]{0:T(128)S(1)}, s32[128]{0:T(128)}, u32[]{:S(2)}) copy-start(s32[128]{0:T(128)} %get-tuple-element.14) | copy-start | bytes 1540
  45.7 5.4 %copy-start.3 = (f32[128]{0:T(128)S(1)}, f32[128]{0:T(128)}, u32[]{:S(2)}) copy-start(f32[128]{0:T(128)} %subtract_multiply_fusion) | copy-start | bytes 1540
  45.7 5.4 %copy-start.4 = (pred[128]{0:T(512)(128)(4,1)S(1)}, pred[128]{0:T(512)(128)(4,1)}, u32[]{:S(2)}) copy-start(pred[128]{0:T(512)(128)(4,1)} %fusion.35) | copy-start | bytes 388
Sparse Core Ops, SparseCore 0:
  159.8 52.4 reduce-scatter.1
where the time goes:
time: 220 us; the launch traced here: 219 us
  blocking collectives  97.3 us (44%)
  waiting for transfers between devices  55.9 us (25%)
  local copies, waits for them, and re-layouts  18.3 us (8%)
  between operations  13.5 us (6%)
  starting transfers between devices  12.7 us (6%)
  other arithmetic  12.3 us (6%)
  matrix products  9.03 us (4%)
    all_to_all x1, blocking collectives, shards(): lax.all_to_all(shaped, 'space', split_axis=0, concat_axis=2, tiled=True)  97.3 us
    reduce_scatter x1, waiting for transfers between devices, shards(): return lax.psum_scatter(arrived, 'tm', scatter_dimension=0, tiled=True)  52.6 us
    ppermute x3, starting transfers between devices, extended(): lax.ppermute(tail, axis, [(i, (i + 1) % count) for i in range(ends)])  10.1 us
    dot_general x1, matrix products, shards(): jnp.dot(coeffs, gradients.reshape(samples, 2 * rows_dev * span_cells), pr...  6.2 us
    another operation x1, local copies, waits for them, and re-layouts, spatial_gradients(): return jnp.stack((along_rows, along_span), axis=1)  5.36 us
    another operation x2, other arithmetic, spatial_gradients(): return jnp.stack((along_rows, along_span), axis=1)  5 us
  transfers between devices with their start and end apart: 7, of which 3 were waited for; matrix products, arithmetic and copies ran while one was open for 6% of the time, Pallas kernels for 0%

commit v1 on v0

--- a/solution.py
+++ b/solution.py
@@ -44,16 +44,9 @@
     return waves * weighting[None, :]
 
 
-def spatial_gradients(fields, metric):
-    row_padded = extended(fields, (("space", 1),), 1, False)
-    along_rows = 0.5 * metric[None, :, None] * (row_padded[:, 2:, :] - row_padded[:, :-2, :])
-    span_padded = extended(fields, (("span", 2),), 1, True)
-    along_span = 0.5 * (span_padded[:, :, 2:] - span_padded[:, :, :-2])
-    return jnp.stack((along_rows, along_span), axis=1)
-
-
 def shards(snapshots, lagrange_weights, source_start, band_len, band_list, row_metric):
     tm_index = lax.axis_index("tm")
+    n_tm, n_space = lax.axis_size("tm"), lax.axis_size("space")
     steps_dev, rows_dev, span_cells = snapshots.shape
     samples = source_start.shape[0]
     reach = extended(snapshots, (("tm", 0),), HALO, False)
@@ -66,20 +59,25 @@
     interp_matrix = jnp.sum(
         jnp.where(selected, lagrange_weights[:, :, None], jnp.float32(0.0)), axis=1
     )
-    flat_reach = reach.reshape(reach_len, rows_dev * span_cells)
     total_rows = 2 * NL * BW
-    positions = jnp.arange(total_rows)
+    own = total_rows // (n_tm * n_space)
+    positions = jnp.arange(total_rows).reshape(n_space, n_tm, own).transpose(1, 0, 2).reshape(-1)
     coeffs = dft_rows(band_list, positions, tm_index * samples, samples)
-    interpolated = jnp.dot(interp_matrix, flat_reach, precision=lax.Precision.HIGHEST)
-    gradients = spatial_gradients(interpolated.reshape(samples, rows_dev, span_cells), row_metric)
-    partial_value = jnp.dot(
-        coeffs,
-        gradients.reshape(samples, 2 * rows_dev * span_cells),
+    combined = jnp.dot(coeffs, interp_matrix, precision=lax.Precision.HIGHEST)
+    partial = jnp.dot(
+        combined,
+        reach.reshape(reach_len, rows_dev * span_cells),
         precision=lax.Precision.HIGHEST,
     )
-    shaped = partial_value.reshape(total_rows, 2, rows_dev, span_cells)
-    arrived = lax.all_to_all(shaped, "space", split_axis=0, concat_axis=2, tiled=True)
-    return lax.psum_scatter(arrived, "tm", scatter_dimension=0, tiled=True)
+    summed = lax.psum_scatter(partial, "tm", scatter_dimension=0, tiled=True)
+    summed = summed.reshape(n_space * own, rows_dev, span_cells)
+    fields = lax.all_to_all(summed, "space", split_axis=0, concat_axis=1, tiled=True)
+    metric = lax.all_gather(row_metric, "space", tiled=True)
+    row_padded = jnp.pad(fields, ((0, 0), (1, 1), (0, 0)))
+    along_rows = 0.5 * metric[None, :, None] * (row_padded[:, 2:, :] - row_padded[:, :-2, :])
+    span_padded = extended(fields, (("span", 2),), 1, True)
+    along_span = 0.5 * (span_padded[:, :, 2:] - span_padded[:, :, :-2])
+    return jnp.stack((along_rows, along_span), axis=1)
 
 
 def solution(mesh):

time: 220 us -> 105 us (0.48)
  blocking collectives: 97.3 us -> 21.8 us
  waiting for transfers between devices: 55.9 us -> 42 us
  local copies, waits for them, and re-layouts: 18.3 us -> 6.28 us
  other arithmetic: 12.3 us -> 5.39 us
  matrix products: 9.03 us -> 3.72 us
    all_to_all x1 -> x0, blocking collectives: 97.3 us -> none  [shards(): lax.all_to_all(shaped, 'space', split_axis=0, concat_axis=2, tiled=True)]
    unnamed x0 -> x1, blocking collectives: none -> 21.8 us
    reduce_scatter x1, waiting for transfers between devices: 52.6 us -> 32.3 us  [shards(): summed = lax.psum_scatter(partial, 'tm', scatter_dimension=0, tiled=True)]
    another operation x1 -> x0, local copies, waits for them, and re-layouts: 5.36 us -> none  [spatial_gradients(): return jnp.stack((along_rows, along_span), axis=1)]
    dot_general x2, matrix products: 9.03 us -> 3.72 us  [the longest x1 3.18 us: shards(): jnp.dot(combined, reach.reshape(reach_len, rows_dev * span_cells), precis...]
    ppermute x3 -> x2, starting transfers between devices: 10.1 us -> 5.36 us  [extended(): lax.ppermute(tail, axis, [(i, (i + 1) % count) for i in range(ends)])]
    unnamed x10 -> x11, local copies, waits for them, and re-layouts: 0.02 us -> 4.74 us
    all_to_all x0 -> x1, starting transfers between devices: none -> 4.59 us  [shards(): lax.all_to_all(summed, 'space', split_axis=0, concat_axis=1, tiled=True)]
  transfers between devices with their start and end apart: 7 -> 6, of which waited for: 3 -> 6; matrix products, arithmetic and copies ran while one was open for 6% -> 4% of each run, Pallas kernels for 0% -> 0%
where the time goes in v1:
time: 105 us
  waiting for transfers between devices  42 us (40%)
  blocking collectives  21.8 us (21%)
  between operations  14.1 us (13%)
  starting transfers between devices  11.3 us (11%)
  local copies, waits for them, and re-layouts  6.28 us (6%)
  other arithmetic  5.39 us (5%)
  matrix products  3.72 us (4%)
    reduce_scatter x1, waiting for transfers between devices, shards(): summed = lax.psum_scatter(partial, 'tm', scatter_dimension=0, tiled=True)  32.3 us
    unnamed x1, blocking collectives  21.8 us
    ppermute x2, waiting for transfers between devices, extended(): lax.ppermute(head, axis, [((i + 1) % count, i) for i in range(ends)])  5.52 us
    ppermute x2, starting transfers between devices, extended(): lax.ppermute(tail, axis, [(i, (i + 1) % count) for i in range(ends)])  5.36 us
    unnamed x11, local copies, waits for them, and re-layouts  4.74 us
    all_to_all x1, starting transfers between devices, shards(): lax.all_to_all(summed, 'space', split_axis=0, concat_axis=1, tiled=True)  4.59 us
    dot_general x1, matrix products, shards(): jnp.dot(combined, reach.reshape(reach_len, rows_dev * span_cells), precis...  3.18 us
    all_to_all x1, waiting for transfers between devices, shards(): lax.all_to_all(summed, 'space', split_axis=0, concat_axis=1, tiled=True)  2.73 us
  transfers between devices with their start and end apart: 6, of which 6 were waited for; matrix products, arithmetic and copies ran while one was open for 4% of the time, Pallas kernels for 0%

profile of v1, /device:TPU:0, one launch (start us, length us, event | category | flops | bytes accessed | tf_op | source)
XLA Modules:
  0.0 104.5 jit_solution(15764756894311047526)
XLA Ops:
  6.5 0.0 copy-start
  6.5 0.0 reduce-scatter.2.cloned.1.call-start
  6.5 1.2 %fusion.34 = (f32[16,16,256]{2,1,0:T(8,128)S(1)}, f32[16,16,256]{2,1,0:T(8,128)S(1)}) fusion(f32[80,16,256]{2,1,0:T(8,128)} %param.6), kind=kLoop, calls=%fused_computation.64 | loop fusion | bytes 1048576 | tf_op jit(solution)/shard_map/slice | solution.py:19
  7.7 4.9 %collective-permute-start = (f32[16,16,256]{2,1,0:T(8,128)S(1)}, f32[16,16,256]{2,1,0:T(8,128)S(1)}, u32[]{:S(2)}, u32[]{:S(2)}) collective-permute-start(f32[16,16,256]{2,1,0:T(8,128)S(1)} %get-tuple-element.7), channel_id=1, source_target_pairs={{0,2},{1,3},{4,6},{5,7},{8,10},{9,11},{12,14},{13,15},{16,18},{17,... | collective-permute-start | bytes 786440 | tf_op jit(solution)/shard_map/ppermute | solution.py:22
  12.6 1.3 %collective-permute-start.1 = (f32[16,16,256]{2,1,0:T(8,128)S(1)}, f32[16,16,256]{2,1,0:T(8,128)S(1)}, u32[]{:S(2)}, u32[]{:S(2)}) collective-permute-start(f32[16,16,256]{2,1,0:T(8,128)S(1)} %get-tuple-element.8), channel_id=1, source_target_pairs={{2,0},{3,1},{6,4},{7,5},{10,8},{11,9},{14,12},{15,13},{18,16},{19,... | collective-permute-start | bytes 786440 | tf_op jit(solution)/shard_map/ppermute | solution.py:24
  13.9 0.1 reshape.208
  14.0 0.7 iota_compare_fusion.1
  14.7 0.7 add_subtract_fusion
  15.3 0.7 select_reduce_fusion.1
  16.1 0.8 select_reduce_fusion
  16.9 0.1 subtract_multiply_fusion
  16.9 0.5 fusion.10
  17.5 0.6 collective-permute-done
  18.1 4.1 %collective-permute-done.1 = f32[16,16,256]{2,1,0:T(8,128)S(1)} collective-permute-done((f32[16,16,256]{2,1,0:T(8,128)S(1)}, f32[16,16,256]{2,1,0:T(8,128)S(1)}, u32[]{:S(2)}, u32[]{:S(2)}) %collective-permute-start.1) | collective-permute-done | bytes 262176 | tf_op jit(solution)/shard_map/ppermute | solution.py:24
  22.2 0.0 copy-done
  22.2 0.1 pad_maximum_fusion.1
  22.4 1.4 %copy.12 = f32[14,8,16,256]{3,1,2,0:T(8,128)S(1)} copy(f32[14,8,16,256]{3,2,1,0:T(8,128)S(1)} %bitcast.20) | data formatting | bytes 3670016
  23.8 3.2 %fusion.36 = f32[128,4096]{1,0:T(8,128)} fusion(f32[128,112]{1,0:T(8,128)S(1)} %fusion.10, f32[112,4096]{1,0:T(8,128)S(1)} %bitcast.21), kind=kOutput, calls=%fused_computation.66 | convolution fusion | flops 704643072 | bytes 3989504 | tf_op jit(solution)/shard_map/dot_general | solution.py:67
  26.9 0.0 reduce-scatter.2.cloned.1.call-update
  27.0 32.3 %reduce-scatter.2.cloned.1.call-done = f32[64,4096]{1,0:T(8,128)} async-done(((f32[128,4096]{1,0:T(8,128)}), f32[64,4096]{1,0:T(8,128)}) %reduce-scatter.2.cloned.1.call-update) | async-done | bytes 1048592 | tf_op jit(solution)/shard_map/reduce_scatter | solution.py:72
  59.3 0.0 copy-start.2
  59.3 0.0 copy-start.1
  59.3 2.5 %copy.13 = f32[8,8,16,256]{3,2,1,0:T(8,128)} copy(f32[8,8,16,256]{3,1,2,0:T(8,128)} %bitcast.23) | data formatting | bytes 2097152
  61.8 4.6 %all-to-all-start = ((f32[64,16,256]{2,1,0:T(8,128)}), f32[64,16,256]{2,1,0:T(8,128)S(1)}, u32[]{:S(2)}, u32[]{:S(2)}) async-start(f32[64,16,256]{2,1,0:T(8,128)} %bitcast.12), calls=%async_computation.1 | async-start | bytes 2097152 | tf_op jit(solution)/shard_map/all_to_all | solution.py:74
  66.4 0.0 copy-done.2
  66.4 0.6 dynamic-slice
  67.6 0.0 copy-done.1
  67.6 0.2 dynamic-update-slice
  67.8 21.8 %all-reduce.1 = f32[64]{0:T(128)S(1)} all-reduce(f32[64]{0:T(128)S(1)} %dynamic-update-slice), channel_id=1, replica_groups=mesh['blocks'=2,'space'=4,'tm'=2,'span'=2] {'space'}, use_global_device_ids=true, to_apply=%add.1 | all-reduce | flops 64 | bytes 512
  89.6 2.7 %all-to-all-done = f32[64,16,256]{2,1,0:T(8,128)S(1)} async-done(((f32[64,16,256]{2,1,0:T(8,128)}), f32[64,16,256]{2,1,0:T(8,128)S(1)}, u32[]{:S(2)}, u32[]{:S(2)}) %all-to-all-start) | async-done | bytes 1048608 | tf_op jit(solution)/shard_map/all_to_all | solution.py:74
  92.3 0.1 copy.10
  92.4 0.2 fusion.35
  92.6 0.1 collective-permute-start.2
  92.7 0.5 collective-permute-start.3
  93.2 1.4 %collective-permute-done.2 = f32[16,64,1]{2,1,0:T(8,128)S(1)} collective-permute-done((f32[16,64,1]{2,1,0:T(8,128)S(1)}, f32[16,64,1]{2,1,0:T(8,128)S(1)}, u32[]{:S(2)}, u32[]{:S(2)}) %collective-permute-start.2) | collective-permute-done | bytes 4128 | tf_op jit(solution)/shard_map/ppermute | solution.py:24
  94.6 0.7 collective-permute-done.3
  95.4 0.8 fusion.2
  96.2 1.5 %pad_maximum_fusion = f32[16,2,64,256]{3,2,1,0:T(8,128)} fusion(f32[16,1,64,256]{3,2,1,0:T(8,128)S(1)} %get-tuple-element.10, f32[16,1,64,256]{3,2,1,0:T(8,128)S(1)} %get-tuple-element.9), kind=kLoop, calls=%fused_computation | loop fusion | flops 524288 | bytes 4194304 | tf_op jit(solution)/shard_map/stack | solution.py:80
  (6 shorter events, 0.1 us)
Async XLA Ops:
  6.5 15.7 %copy-start = (f32[80,16,256]{2,1,0:T(8,128)S(1)}, f32[80,16,256]{2,1,0:T(8,128)}, u32[]{:S(2)}) copy-start(f32[80,16,256]{2,1,0:T(8,128)} %param.6) | copy-start | bytes 3932164
  6.5 52.7 %reduce-scatter.2.cloned.1.call-start = ((), (), s32[]{:S(2)}) async-start(), calls=%async_computation.2 | async-start | bytes 3145728 | tf_op jit(solution)/shard_map/reduce_scatter | solution.py:72
  7.7 10.4 %collective-permute-start = (f32[16,16,256]{2,1,0:T(8,128)S(1)}, f32[16,16,256]{2,1,0:T(8,128)S(1)}, u32[]{:S(2)}, u32[]{:S(2)}) collective-permute-start(f32[16,16,256]{2,1,0:T(8,128)S(1)} %get-tuple-element.7), channel_id=1, source_target_pairs={{0,2},{1,3},{4,6},{5,7},{8,10},{9,11},{12,14},{13,15},{16,18},{17,... | collective-permute-start | bytes 786440 | tf_op jit(solution)/shard_map/ppermute | solution.py:22
  12.6 9.7 %collective-permute-start.1 = (f32[16,16,256]{2,1,0:T(8,128)S(1)}, f32[16,16,256]{2,1,0:T(8,128)S(1)}, u32[]{:S(2)}, u32[]{:S(2)}) collective-permute-start(f32[16,16,256]{2,1,0:T(8,128)S(1)} %get-tuple-element.8), channel_id=1, source_target_pairs={{2,0},{3,1},{6,4},{7,5},{10,8},{11,9},{14,12},{15,13},{18,16},{19,... | collective-permute-start | bytes 786440 | tf_op jit(solution)/shard_map/ppermute | solution.py:24
  59.3 7.1 %copy-start.2 = (u32[32]{0:T(128)S(1)}, u32[32]{0:T(128)}, u32[]{:S(2)}) copy-start(u32[32]{0:T(128)} %constant.95) | copy-start | bytes 388
  59.3 8.3 %copy-start.1 = (f32[16]{0:T(128)S(1)}, f32[16]{0:T(128)}, u32[]{:S(2)}) copy-start(f32[16]{0:T(128)} %param.11) | copy-start | bytes 196
  61.8 30.5 %all-to-all-start = ((f32[64,16,256]{2,1,0:T(8,128)}), f32[64,16,256]{2,1,0:T(8,128)S(1)}, u32[]{:S(2)}, u32[]{:S(2)}) async-start(f32[64,16,256]{2,1,0:T(8,128)} %bitcast.12), calls=%async_computation.1 | async-start | bytes 2097152 | tf_op jit(solution)/shard_map/all_to_all | solution.py:74
  92.6 2.0 %collective-permute-start.2 = (f32[16,64,1]{2,1,0:T(8,128)S(1)}, f32[16,64,1]{2,1,0:T(8,128)S(1)}, u32[]{:S(2)}, u32[]{:S(2)}) collective-permute-start(f32[16,64,1]{2,1,0:T(8,128)S(1)} %get-tuple-element.11), channel_id=1, source_target_pairs={{1,0},{0,1},{3,2},{2,3},{5,4},{4,5},{7,6},{6,7},{9,8},{8,9},{11,10... | collective-permute-start | bytes 12296 | tf_op jit(solution)/shard_map/ppermute | solution.py:24
  92.7 2.6 %collective-permute-start.3 = (f32[16,64,1]{2,1,0:T(8,128)S(1)}, f32[16,64,1]{2,1,0:T(8,128)S(1)}, u32[]{:S(2)}, u32[]{:S(2)}) collective-permute-start(f32[16,64,1]{2,1,0:T(8,128)S(1)} %get-tuple-element.12), channel_id=1, source_target_pairs={{0,1},{1,0},{2,3},{3,2},{4,5},{5,4},{6,7},{7,6},{8,9},{9,8},{10,11... | collective-permute-start | bytes 12296 | tf_op jit(solution)/shard_map/ppermute | solution.py:22
Sparse Core Ops, SparseCore 0:
  27.1 32.1 reduce-scatter.1

commit v2 on v1

v2 whole, which is shorter than its diff:
```python
import functools
import math

import jax
import jax.numpy as jnp
from jax import lax
from jax.experimental import pallas as pl
from jax.experimental.pallas import tpu as pltpu
from jax.sharding import PartitionSpec as P

NT = 256
BW = 8
NL = 8
SLOTS = 6
LANES = 128
PAD = 8
CHUNKS = 4
MESH = pl.DeviceIdType.MESH
HIGHEST = lax.Precision.HIGHEST


def cosine(phase):
    folded = NT // 4 - jnp.minimum(phase, NT - phase)
    u = folded.astype(jnp.float32) * (2.0 * math.pi / NT)
    square = u * u
    total = jnp.full_like(u, 1.0 / math.factorial(13))
    for order in (11, 9, 7, 5, 3, 1):
        sign = 1.0 if order % 4 == 1 else -1.0
        total = total * square + sign / math.factorial(order)
    return total * u


def kernel(
    dims,
    x_ref,
    w_ref,
    start_ref,
    len_ref,
    band_ref,
    metric_ref,
    out_ref,
    packed,
    metrics,
    mixing,
    fields,
    arrived,
    final,
    edges,
    pk_send,
    pk_recv,
    mt_send,
    mt_recv,
    x_send,
    x_recv,
    z_send,
    z_recv,
    e_send,
    e_recv,
):
    n_tm, n_space, steps, rows, cells, samples, own, chunks = dims
    per = own // chunks
    total = 2 * NL * BW
    tm, space, span = lax.axis_index("tm"), lax.axis_index("space"), lax.axis_index("span")
    group = n_space * per
    tiles = cells // LANES
    pitch = tiles * rows
    flat = fields.reshape(total * pitch, LANES)

    def peer_tm(d):
        return {"tm": lax.rem(tm + d, n_tm)}

    def peer_space(d):
        return {"space": lax.rem(space + d, n_space)}

    other = {"span": 1 - span}

    barrier = pltpu.get_barrier_semaphore()
    for d in range(1, n_tm):
        pl.semaphore_signal(barrier, inc=1, device_id=peer_tm(d), device_id_type=MESH)
    for d in range(1, n_space):
        pl.semaphore_signal(barrier, inc=1, device_id=peer_space(d), device_id_type=MESH)
    pl.semaphore_signal(barrier, inc=1, device_id=other, device_id_type=MESH)

    packed[tm] = jnp.zeros((8, LANES), jnp.float32)
    packed[tm, 0:SLOTS, 0:samples] = w_ref[...]
    packed[tm, 6:7, 0:samples] = start_ref[...].astype(jnp.float32)
    packed[tm, 7:8, 0:samples] = len_ref[...].astype(jnp.float32)
    square = (rows, rows)
    diagonal = lax.broadcasted_iota(jnp.int32, square, 0) == lax.broadcasted_iota(
        jnp.int32, square, 1
    )
    column = jnp.sum(
        jnp.where(diagonal, jnp.broadcast_to(metric_ref[...], square), 0.0), axis=1, keepdims=True
    )
    mine = pl.ds(pl.multiple_of(space * rows, 8), rows)
    metrics[mine, :] = jnp.broadcast_to(0.5 * column, (rows, LANES))

    pl.semaphore_wait(barrier, n_tm - 1 + n_space - 1 + 1)

    started = []
    pk_copies = []
    for d in range(1, n_tm):
        copy = pltpu.make_async_remote_copy(
            packed.at[tm], packed.at[tm], pk_send.at[d - 1], pk_recv.at[d - 1],
            device_id=peer_tm(d), device_id_type=MESH,
        )
        copy.start()
        pk_copies.append(copy)
    mt_copies = []
    for d in range(1, n_space):
        copy = pltpu.make_async_remote_copy(
            metrics.at[mine, :], metrics.at[mine, :], mt_send.at[d - 1], mt_recv.at[d - 1],
            device_id=peer_space(d), device_id_type=MESH,
        )
        copy.start()
        mt_copies.append(copy)

    for g in range(own):
        for v in range(tiles):
            final[g, v, 0:PAD, :] = jnp.zeros((PAD, LANES), jnp.float32)
            final[g, v, PAD + n_space * rows :, :] = jnp.zeros((PAD, LANES), jnp.float32)

    p = lax.broadcasted_iota(jnp.int32, (total, LANES), 0)
    lane = lax.broadcasted_iota(jnp.int32, (total, LANES), 1)
    low = lax.rem(p, per)
    i = lax.rem(lax.div(p, per), n_space)
    j = lax.rem(lax.div(p, per * n_space), n_tm)
    c = lax.div(p, per * n_space * n_tm)
    g = (i * n_tm + j) * own + c * per + low
    listed = g >> 1
    band_pos = lax.div(listed, BW)
    band = jnp.zeros_like(p)
    for b in range(NL):
        band = jnp.where(band_pos == b, band_ref[b], band)
    frequency = band * BW + lax.rem(listed, BW)
    quarter = (NT // 4) * (g & 1)

    def dft(q):
        t = q * samples + lane
        phase = (frequency * t + quarter) & (NT - 1)
        window = 0.5 - 0.5 * cosine(t & (NT - 1))
        return cosine(phase) * (window / math.sqrt(NT))

    waves = [dft(lax.rem(tm + n_tm - d, n_tm)) for d in range(n_tm)]

    step = tm * steps + lax.broadcasted_iota(jnp.int32, (steps, LANES), 0)
    mixed = None
    for d in range(n_tm):
        q = lax.rem(tm + n_tm - d, n_tm)
        if d > 0:
            pk_copies[d - 1].wait_recv()
        table = packed[q]
        slot = step - table[6:7].astype(jnp.int32)
        slot = jnp.where(slot < table[7:8].astype(jnp.int32), slot, -1)
        weights = jnp.zeros((steps, LANES), jnp.float32)
        for s in range(SLOTS):
            weights = jnp.where(slot == s, table[s : s + 1], weights)
        term = lax.dot_general(
            waves[d], weights, (((1,), (1,)), ((), ())),
            precision=HIGHEST, preferred_element_type=jnp.float32,
        )
        mixed = term if mixed is None else mixed + term
    mixing[...] = mixed

    rows_per = n_tm * group
    x_copies, z_copies, e_copies = {}, {}, {}

    def start_x(c):
        left = mixing[c * rows_per : (c + 1) * rows_per, :]

        def body(r, carry):
            from_row = lax.div(r, 8) * (8 * tiles) + lax.rem(r, 8)
            right = jnp.concatenate(
                [x_ref[pl.ds(from_row + 8 * v, steps, stride=pitch), :] for v in range(tiles)], axis=1
            )
            value = jnp.dot(left, right, precision=HIGHEST, preferred_element_type=jnp.float32)
            for v in range(tiles):
                flat[pl.ds(c * rows_per * pitch + v * rows + r, rows_per, stride=pitch), :] = value[
                    :, v * LANES : (v + 1) * LANES
                ]
            return carry

        lax.fori_loop(0, rows, body, 0, unroll=4)
        x_copies[c] = []
        for d in range(1, n_tm):
            to = lax.rem(tm + d, n_tm)
            copy = pltpu.make_async_remote_copy(
                fields.at[pl.ds((c * n_tm + to) * group, group)],
                arrived.at[c, d - 1],
                x_send.at[c, d - 1], x_recv.at[c, d - 1],
                device_id=peer_tm(d), device_id_type=MESH,
            )
            copy.start()
            x_copies[c].append(copy)

    def start_z(c):
        for copy in x_copies[c]:
            copy.wait_recv()
        base = (c * n_tm + tm) * group

        def body(k, carry):
            value = fields[base + k]
            for d in range(1, n_tm):
                value = value + arrived[c, d - 1, k]
            fields[base + k] = value
            return carry

        lax.fori_loop(0, group, body, 0, unroll=min(4, group))
        z_copies[c] = []
        there = pl.ds(pl.multiple_of(PAD + space * rows, 8), rows)
        for d in range(1, n_space):
            to = lax.rem(space + d, n_space)
            copy = pltpu.make_async_remote_copy(
                fields.at[pl.ds(base + to * per, per)],
                final.at[pl.ds(c * per, per), pl.ds(0, tiles), there, :],
                z_send.at[c, d - 1], z_recv.at[c, d - 1],
                device_id=peer_space(d), device_id_type=MESH,
            )
            copy.start()
            z_copies[c].append(copy)
        for k in range(per):
            final[c * per + k, 0:tiles, there, :] = fields[base + space * per + k]

    inner = pl.ds(PAD, n_space * rows)

    def start_e(c):
        for copy in z_copies[c]:
            copy.wait_recv()
        first = lax.broadcasted_iota(jnp.int32, (n_space * rows, LANES), 1) == 0
        for k in range(per):
            g = c * per + k
            edges[g] = jnp.where(
                first, final[g, 0, inner, :], final[g, tiles - 1, inner, :]
            )
        copy = pltpu.make_async_remote_copy(
            edges.at[pl.ds(c * per, per)],
            final.at[pl.ds(c * per, per), tiles, inner, :],
            e_send.at[c], e_recv.at[c],
            device_id=other, device_id_type=MESH,
        )
        copy.start()
        e_copies[c] = copy

    def finish(c):
        e_copies[c].wait_recv()
        scale = metrics[...]
        for k in range(per):
            g = c * per + k
            for v in range(tiles):
                above = final[g, v, PAD + 1 : PAD + 1 + n_space * rows, :]
                below = final[g, v, PAD - 1 : PAD - 1 + n_space * rows, :]
                out_ref[g, 0, :, v * LANES : (v + 1) * LANES] = scale * (above - below)
            ring = jnp.concatenate([final[g, v, inner, :] for v in range(tiles + 1)], axis=1)
            after = pltpu.roll(ring, cells + LANES - 1, 1)
            before = pltpu.roll(ring, 1, 1)
            out_ref[g, 1] = 0.5 * (after - before)[:, 0:cells]

    for s in range(chunks + 3):
        if s < chunks:
            start_x(s)
        if 0 <= s - 1 < chunks:
            start_z(s - 1)
        if s == 2:
            for copy in mt_copies:
                copy.wait_recv()
        if 0 <= s - 2 < chunks:
            start_e(s - 2)
        if 0 <= s - 3 < chunks:
            finish(s - 3)

    for copy in pk_copies + mt_copies:
        copy.wait_send()
    for c in range(chunks):
        for copy in x_copies[c] + z_copies[c] + [e_copies[c]]:
            copy.wait_send()


def shards(snapshots, lagrange_weights, source_start, band_len, band_list, row_metric):
    n_tm, n_space = lax.axis_size("tm"), lax.axis_size("space")
    steps, rows, cells = snapshots.shape
    samples = source_start.shape[0]
    total = 2 * NL * BW
    own = total // (n_tm * n_space)
    chunks = math.gcd(own, CHUNKS)
    per = own // chunks
    dims = (n_tm, n_space, steps, rows, cells, samples, own, chunks)
    vmem = pl.BlockSpec(memory_space=pltpu.VMEM)
    f32 = jnp.float32
    dma = pltpu.SemaphoreType.DMA
    return pl.pallas_call(
        functools.partial(kernel, dims),
        out_shape=jax.ShapeDtypeStruct((own, 2, n_space * rows, cells), f32),
        in_specs=[vmem, vmem, vmem, vmem, pl.BlockSpec(memory_space=pltpu.SMEM), vmem],
        out_specs=vmem,
        scratch_shapes=[
            pltpu.VMEM((n_tm, 8, LANES), f32),
            pltpu.VMEM((n_space * rows, LANES), f32),
            pltpu.VMEM((total, steps), f32),
            pltpu.VMEM((total, cells // LANES, rows, LANES), f32),
            pltpu.VMEM((chunks, n_tm - 1, n_space * per, cells // LANES, rows, LANES), f32),
            pltpu.VMEM((own, cells // LANES + 1, n_space * rows + 2 * PAD, LANES), f32),
            pltpu.VMEM((own, n_space * rows, LANES), f32),
            dma((n_tm - 1,)),
            dma((n_tm - 1,)),
            dma((n_space - 1,)),
            dma((n_space - 1,)),
            dma((chunks, n_tm - 1)),
            dma((chunks, n_tm - 1)),
            dma((chunks, n_space - 1)),
            dma((chunks, n_space - 1)),
            dma((chunks,)),
            dma((chunks,)),
        ],
        compiler_params=pltpu.CompilerParams(
            collective_id=0, has_side_effects=True, vmem_limit_bytes=32 * 1024 * 1024
        ),
    )(
        snapshots.reshape(steps, rows // 8, 8, cells // LANES, LANES)
        .swapaxes(2, 3)
        .reshape(steps * rows * (cells // LANES), LANES),
        lagrange_weights.T,
        source_start.reshape(1, samples),
        band_len.reshape(1, samples),
        band_list,
        row_metric.reshape(1, rows),
    )


def solution(mesh):
    placed = (
        P(("blocks", "tm"), "space", "span"),
        P(("blocks", "tm"), None),
        P(("blocks", "tm")),
        P(("blocks", "tm")),
        P(),
        P("space"),
    )
    return jax.shard_map(
        shards,
        mesh=mesh,
        in_specs=placed,
        out_specs=P(("blocks", "space", "tm"), None, None, "span"),
        check_vma=False,
    )
```

time: 105 us -> 47.3 us (0.45)
  waiting for transfers between devices: 42 us -> 0 us
  Pallas kernels: 0 us -> 40.9 us
  blocking collectives: 21.8 us -> 0 us
  between operations: 14.1 us -> 0.02 us
  starting transfers between devices: 11.3 us -> 0 us
  other arithmetic: 5.39 us -> 0 us
  matrix products: 3.72 us -> 0 us
    pallas_call x0 -> x1, Pallas kernels: none -> 40.9 us  [shards(): pl.pallas_call(functools.partial(kernel, dims), out_shape=jax.ShapeDtypeS...]
    reduce_scatter x1 -> x0, waiting for transfers between devices: 32.3 us -> none  [shards(): summed = lax.psum_scatter(partial, 'tm', scatter_dimension=0, tiled=True)]
    unnamed x1 -> x0, blocking collectives: 21.8 us -> none
    ppermute x4 -> x0, waiting for transfers between devices: 6.92 us -> none  [the longest x2 5.52 us: extended(): lax.ppermute(head, axis, [((i + 1) % count, i) for i in range(ends)])]
    ppermute x4 -> x0, starting transfers between devices: 6.72 us -> none  [the longest x2 5.36 us: extended(): lax.ppermute(tail, axis, [(i, (i + 1) % count) for i in range(ends)])]
    all_to_all x1 -> x0, starting transfers between devices: 4.59 us -> none  [shards(): lax.all_to_all(summed, 'space', split_axis=0, concat_axis=1, tiled=True)]
    dot_general x2 -> x0, matrix products: 3.72 us -> none  [the longest x1 3.18 us: shards(): jnp.dot(combined, reach.reshape(reach_len, rows_dev * span_cells), precis...]
    all_to_all x1 -> x0, waiting for transfers between devices: 2.73 us -> none  [shards(): lax.all_to_all(summed, 'space', split_axis=0, concat_axis=1, tiled=True)]
  transfers between devices with their start and end apart: 6 -> 0, of which waited for: 6 -> 0; matrix products, arithmetic and copies ran while one was open for 4% -> 0% of each run, Pallas kernels for 0% -> 0%
where the time goes in v2:
time: 47.3 us; the launch traced here: 46.9 us
  Pallas kernels  40.9 us (86%)
  local copies, waits for them, and re-layouts  5.94 us (13%)
    pallas_call x1, Pallas kernels, shards(): pl.pallas_call(functools.partial(kernel, dims), out_shape=jax.ShapeDtypeS...  40.9 us
    unnamed x13, local copies, waits for them, and re-layouts  5.94 us

profile of v2, /device:TPU:0, one launch (start us, length us, event | category | flops | bytes accessed | tf_op | source)
XLA Modules:
  0.0 46.9 jit_solution(15335922050539664054)
XLA Ops:
  0.0 0.0 copy-start
  0.0 1.3 %copy-done = f32[80,16,256]{2,1,0:T(8,128)S(1)} copy-done((f32[80,16,256]{2,1,0:T(8,128)S(1)}, f32[80,16,256]{2,1,0:T(8,128)}, u32[]{:S(2)}) %copy-start) | copy-done | bytes 1310744
  1.3 0.0 copy-start.1
  1.3 0.7 %copy-done.1 = f32[128,6]{0,1:T(8,128)S(1)} copy-done((f32[128,6]{0,1:T(8,128)S(1)}, f32[128,6]{0,1:T(8,128)}, u32[]{:S(2)}) %copy-start.1) | copy-done | bytes 3096
  2.0 0.0 copy-start.2
  2.0 0.7 %copy-done.2 = s32[128]{0:T(128)S(1)} copy-done((s32[128]{0:T(128)S(1)}, s32[128]{0:T(128)}, u32[]{:S(2)}) %copy-start.2) | copy-done | bytes 536
  2.7 0.0 copy-start.3
  2.7 0.7 %copy-done.3 = s32[128]{0:T(128)S(1)} copy-done((s32[128]{0:T(128)S(1)}, s32[128]{0:T(128)}, u32[]{:S(2)}) %copy-start.3) | copy-done | bytes 536
  3.3 0.0 copy-start.4
  3.3 0.7 %copy-done.4 = s32[8]{0:T(128)S(1)} copy-done((s32[8]{0:T(128)S(1)}, s32[8]{0:T(128)}, u32[]{:S(2)}) %copy-start.4) | copy-done | bytes 56
  4.0 0.0 copy-start.5
  4.0 0.7 %copy-done.5 = f32[16]{0:T(128)S(1)} copy-done((f32[16]{0:T(128)S(1)}, f32[16]{0:T(128)}, u32[]{:S(2)}) %copy-start.5) | copy-done | bytes 88
  4.6 40.9 %shard_map.64 = f32[16,2,64,256]{3,2,1,0:T(8,128)S(1)} custom-call(f32[2560,128]{1,0:T(8,128)S(1)} %bitcast.9, f32[6,128]{1,0:T(8,128)S(1)} %bitcast.10, s32[1,128]{1,0:T(1,128)S(1)} %bitcast.11, s32[1,128]{1,0:T(1,128)S(1)} %bitcast.12, s32[8]{0:T(128)S(1)} %copy-done.4, f32[1,16]{1,0:T(1,128)S(1)} %bitcast.13), custom_call_target="tpu_custom_call" | custom-call | tf_op jit(solution)/shard_map/pallas_call | solution.py:290
  45.5 1.3 %copy.8 = f32[16,2,64,256]{3,2,1,0:T(8,128)} copy(f32[16,2,64,256]{3,2,1,0:T(8,128)S(1)} %shard_map.64) | data formatting | bytes 4194304
Async XLA Ops:
  0.0 1.3 %copy-start = (f32[80,16,256]{2,1,0:T(8,128)S(1)}, f32[80,16,256]{2,1,0:T(8,128)}, u32[]{:S(2)}) copy-start(f32[80,16,256]{2,1,0:T(8,128)} %param.6) | copy-start | bytes 3932164
  1.3 0.7 %copy-start.1 = (f32[128,6]{0,1:T(8,128)S(1)}, f32[128,6]{0,1:T(8,128)}, u32[]{:S(2)}) copy-start(f32[128,6]{0,1:T(8,128)} %param.7) | copy-start | bytes 9220
  2.0 0.7 %copy-start.2 = (s32[128]{0:T(128)S(1)}, s32[128]{0:T(128)}, u32[]{:S(2)}) copy-start(s32[128]{0:T(128)} %param.8) | copy-start | bytes 1540
  2.7 0.7 %copy-start.3 = (s32[128]{0:T(128)S(1)}, s32[128]{0:T(128)}, u32[]{:S(2)}) copy-start(s32[128]{0:T(128)} %param.9) | copy-start | bytes 1540
  3.3 0.7 %copy-start.4 = (s32[8]{0:T(128)S(1)}, s32[8]{0:T(128)}, u32[]{:S(2)}) copy-start(s32[8]{0:T(128)} %band_ref.1) | copy-start | bytes 100
  4.0 0.7 %copy-start.5 = (f32[16]{0:T(128)S(1)}, f32[16]{0:T(128)}, u32[]{:S(2)}) copy-start(f32[16]{0:T(128)} %param.11) | copy-start | bytes 196

commit v3 on v2

--- a/solution.py
+++ b/solution.py
@@ -14,7 +14,10 @@
 SLOTS = 6
 LANES = 128
 PAD = 8
-CHUNKS = 4
+CHUNKS = 8
+AHEAD = 3
+Z_LAG = 3
+E_LAG = 2
 MESH = pl.DeviceIdType.MESH
 HIGHEST = lax.Precision.HIGHEST
 
@@ -30,15 +33,19 @@
     return total * u
 
 
+def three(value):
+    high = value.astype(jnp.bfloat16).astype(jnp.float32)
+    rest = value - high
+    middle = rest.astype(jnp.bfloat16).astype(jnp.float32)
+    return high, middle, rest - middle
+
+
 def kernel(
     dims,
     x_ref,
-    w_ref,
-    start_ref,
-    len_ref,
-    band_ref,
-    metric_ref,
+    small_ref,
     out_ref,
+    parts,
     packed,
     metrics,
     mixing,
@@ -81,19 +88,28 @@
         pl.semaphore_signal(barrier, inc=1, device_id=peer_space(d), device_id_type=MESH)
     pl.semaphore_signal(barrier, inc=1, device_id=other, device_id_type=MESH)
 
-    packed[tm] = jnp.zeros((8, LANES), jnp.float32)
-    packed[tm, 0:SLOTS, 0:samples] = w_ref[...]
-    packed[tm, 6:7, 0:samples] = start_ref[...].astype(jnp.float32)
-    packed[tm, 7:8, 0:samples] = len_ref[...].astype(jnp.float32)
+    packed[tm] = small_ref[0:8]
     square = (rows, rows)
     diagonal = lax.broadcasted_iota(jnp.int32, square, 0) == lax.broadcasted_iota(
         jnp.int32, square, 1
     )
     column = jnp.sum(
-        jnp.where(diagonal, jnp.broadcast_to(metric_ref[...], square), 0.0), axis=1, keepdims=True
+        jnp.where(diagonal, jnp.broadcast_to(small_ref[8:9, 0:rows], square), 0.0), axis=1, keepdims=True
     )
     mine = pl.ds(pl.multiple_of(space * rows, 8), rows)
     metrics[mine, :] = jnp.broadcast_to(0.5 * column, (rows, LANES))
+
+    def split(r, carry):
+        from_row = lax.div(r, 8) * (8 * tiles) + lax.rem(r, 8)
+        value = jnp.concatenate(
+            [x_ref[pl.ds(from_row + 8 * v, steps, stride=pitch), :] for v in range(tiles)], axis=1
+        )
+        high, middle, low = three(value)
+        for k, part in enumerate((high, middle, low, high, middle, high)):
+            parts[r, k * steps : (k + 1) * steps, :] = part.astype(jnp.bfloat16)
+        return carry
+
+    lax.fori_loop(0, rows, split, 0, unroll=2)
 
     pl.semaphore_wait(barrier, n_tm - 1 + n_space - 1 + 1)
 
@@ -129,9 +145,10 @@
     g = (i * n_tm + j) * own + c * per + low
     listed = g >> 1
     band_pos = lax.div(listed, BW)
+    bands = small_ref[9:10].astype(jnp.int32)
     band = jnp.zeros_like(p)
     for b in range(NL):
-        band = jnp.where(band_pos == b, band_ref[b], band)
+        band = jnp.where(band_pos == b, bands[:, b : b + 1], band)
     frequency = band * BW + lax.rem(listed, BW)
     quarter = (NT // 4) * (g & 1)
 
@@ -156,11 +173,15 @@
         for s in range(SLOTS):
             weights = jnp.where(slot == s, table[s : s + 1], weights)
         term = lax.dot_general(
-            waves[d], weights, (((1,), (1,)), ((), ())),
+            waves[d], jnp.concatenate([weights] * 6, axis=0), (((1,), (1,)), ((), ())),
             precision=HIGHEST, preferred_element_type=jnp.float32,
         )
         mixed = term if mixed is None else mixed + term
-    mixing[...] = mixed
+    high, middle, low = three(mixed)
+    at = lax.broadcasted_iota(jnp.int32, mixed.shape, 1)
+    mixing[...] = jnp.where(
+        at < 3 * steps, high, jnp.where(at < 5 * steps, middle, low)
+    ).astype(jnp.bfloat16)
 
     rows_per = n_tm * group
     x_copies, z_copies, e_copies = {}, {}, {}
@@ -169,11 +190,7 @@
         left = mixing[c * rows_per : (c + 1) * rows_per, :]
 
         def body(r, carry):
-            from_row = lax.div(r, 8) * (8 * tiles) + lax.rem(r, 8)
-            right = jnp.concatenate(
-                [x_ref[pl.ds(from_row + 8 * v, steps, stride=pitch), :] for v in range(tiles)], axis=1
-            )
-            value = jnp.dot(left, right, precision=HIGHEST, preferred_element_type=jnp.float32)
+            value = jnp.dot(left, parts[r], preferred_element_type=jnp.float32)
             for v in range(tiles):
                 flat[pl.ds(c * rows_per * pitch + v * rows + r, rows_per, stride=pitch), :] = value[
                     :, v * LANES : (v + 1) * LANES
@@ -255,18 +272,20 @@
             before = pltpu.roll(ring, 1, 1)
             out_ref[g, 1] = 0.5 * (after - before)[:, 0:cells]
 
-    for s in range(chunks + 3):
+    for c in range(min(AHEAD, chunks)):
+        start_x(c)
+    for s in range(chunks + Z_LAG + E_LAG):
         if s < chunks:
-            start_x(s)
-        if 0 <= s - 1 < chunks:
-            start_z(s - 1)
-        if s == 2:
+            start_z(s)
+        if s + AHEAD < chunks:
+            start_x(s + AHEAD)
+        if s == 1:
             for copy in mt_copies:
                 copy.wait_recv()
-        if 0 <= s - 2 < chunks:
-            start_e(s - 2)
-        if 0 <= s - 3 < chunks:
-            finish(s - 3)
+        if 0 <= s - Z_LAG < chunks:
+            start_e(s - Z_LAG)
+        if 0 <= s - Z_LAG - E_LAG < chunks:
+            finish(s - Z_LAG - E_LAG)
 
     for copy in pk_copies + mt_copies:
         copy.wait_send()
@@ -283,19 +302,29 @@
     own = total // (n_tm * n_space)
     chunks = math.gcd(own, CHUNKS)
     per = own // chunks
+    f32 = jnp.float32
     dims = (n_tm, n_space, steps, rows, cells, samples, own, chunks)
+
+    def line(value):
+        row = value.astype(f32).reshape(-1, value.shape[-1])
+        return jnp.pad(row, ((0, 0), (0, LANES - row.shape[1])))
+
+    small = jnp.concatenate(
+        [line(v) for v in (lagrange_weights.T, source_start, band_len, row_metric, band_list)]
+        + [jnp.zeros((6, LANES), f32)]
+    )
     vmem = pl.BlockSpec(memory_space=pltpu.VMEM)
-    f32 = jnp.float32
     dma = pltpu.SemaphoreType.DMA
     return pl.pallas_call(
         functools.partial(kernel, dims),
         out_shape=jax.ShapeDtypeStruct((own, 2, n_space * rows, cells), f32),
-        in_specs=[vmem, vmem, vmem, vmem, pl.BlockSpec(memory_space=pltpu.SMEM), vmem],
+        in_specs=[vmem, vmem],
         out_specs=vmem,
         scratch_shapes=[
+            pltpu.VMEM((rows, 6 * steps, cells), jnp.bfloat16),
             pltpu.VMEM((n_tm, 8, LANES), f32),
             pltpu.VMEM((n_space * rows, LANES), f32),
-            pltpu.VMEM((total, steps), f32),
+            pltpu.VMEM((total, 6 * steps), jnp.bfloat16),
             pltpu.VMEM((total, cells // LANES, rows, LANES), f32),
             pltpu.VMEM((chunks, n_tm - 1, n_space * per, cells // LANES, rows, LANES), f32),
             pltpu.VMEM((own, cells // LANES + 1, n_space * rows + 2 * PAD, LANES), f32),
@@ -318,11 +347,7 @@
         snapshots.reshape(steps, rows // 8, 8, cells // LANES, LANES)
         .swapaxes(2, 3)
         .reshape(steps * rows * (cells // LANES), LANES),
-        lagrange_weights.T,
-        source_start.reshape(1, samples),
-        band_len.reshape(1, samples),
-        band_list,
-        row_metric.reshape(1, rows),
+        small,
     )
 
 

time: 47.3 us -> 43.9 us (0.928)
  Pallas kernels: 40.9 us -> 38.2 us
  local copies, waits for them, and re-layouts: 5.94 us -> 4.03 us
  other arithmetic: 0 us -> 1.33 us
    unnamed x13 -> x3, local copies, waits for them, and re-layouts: 5.94 us -> 2.64 us
    pallas_call x1, Pallas kernels: 40.9 us -> 38.2 us  [shards(): pl.pallas_call(functools.partial(kernel, dims), out_shape=jax.ShapeDtypeS...]
    reshape x0 -> x2, other arithmetic: none -> 1.33 us  [line(): row = value.astype(f32).reshape(-1, value.shape[-1])]
    concatenate x0 -> x1, local copies, waits for them, and re-layouts: none -> 0.72 us  [shards(): jnp.concatenate([line(v) for v in (lagrange_weights.T, source_start, band...]
    pad x0 -> x2, local copies, waits for them, and re-layouts: none -> 0.67 us  [line(): return jnp.pad(row, ((0, 0), (0, LANES - row.shape[1])))]
where the time goes in v3:
time: 43.9 us; the launch traced here: 43.6 us
  Pallas kernels  38.2 us (87%)
  local copies, waits for them, and re-layouts  4.03 us (9%)
  other arithmetic  1.33 us (3%)
    pallas_call x1, Pallas kernels, shards(): pl.pallas_call(functools.partial(kernel, dims), out_shape=jax.ShapeDtypeS...  38.2 us
    unnamed x3, local copies, waits for them, and re-layouts  2.64 us
    reshape x2, other arithmetic, line(): row = value.astype(f32).reshape(-1, value.shape[-1])  1.33 us

profile of v3, /device:TPU:0, one launch (start us, length us, event | category | flops | bytes accessed | tf_op | source)
XLA Modules:
  0.0 43.6 jit_solution(12268981938960722046)
XLA Ops:
  0.0 0.7 %convert_bitcast_fusion = f32[1,8]{1,0:T(1,128)S(1)} fusion(s32[8]{0:T(128)} %param.10), kind=kLoop, calls=%fused_computation | loop fusion | flops 8 | bytes 64 | tf_op jit(solution)/shard_map/reshape | solution.py:309
  0.7 0.7 %pad.8 = f32[1,128]{1,0:T(1,128)S(1)} pad(f32[1,16]{1,0:T(1,128)} %bitcast.15, f32[]{:T(128)} %constant.1.clone.1), padding=0_0x0_112 | pad | bytes 580 | tf_op jit(solution)/shard_map/jit(_pad)/pad | solution.py:310
  1.3 0.7 %convert_bitcast_fusion.1 = (f32[1,128]{1,0:T(1,128)S(1)}, f32[1,128]{1,0:T(1,128)S(1)}) fusion(s32[128]{0:T(128)} %param.9, s32[128]{0:T(128)} %param.8), kind=kLoop, calls=%fused_computation.1 | loop fusion | flops 256 | bytes 2048 | tf_op jit(solution)/shard_map/reshape | solution.py:309
  2.0 0.7 %concatenate.3.small_ref = f32[16,128]{1,0:T(8,128)S(1)} concatenate(f32[6,128]{1,0:T(8,128)} %bitcast.14, f32[1,128]{1,0:T(1,128)S(1)} %get-tuple-element.6, f32[1,128]{1,0:T(1,128)S(1)} %get-tuple-element.5, f32[1,128]{1,0:T(1,128)S(1)} %pad.8, f32[1,128]{1,0:T(1,128)S(1)} %pad.9, f32[6,128]{1,0:T(8,128)S(1)} %broadcast_in_dim.3), dimensions={0} | concatenate | bytes 16384 | tf_op jit(solution)/shard_map/concatenate | solution.py:312
  2.7 0.0 copy-start
  2.7 1.3 %copy-done = f32[80,16,256]{2,1,0:T(8,128)S(1)} copy-done((f32[80,16,256]{2,1,0:T(8,128)S(1)}, f32[80,16,256]{2,1,0:T(8,128)}, u32[]{:S(2)}) %copy-start) | copy-done | bytes 1310744
  4.0 38.2 %shard_map.64 = f32[16,2,64,256]{3,2,1,0:T(8,128)S(1)} custom-call(f32[2560,128]{1,0:T(8,128)S(1)} %bitcast.13, f32[16,128]{1,0:T(8,128)S(1)} %concatenate.3.small_ref), custom_call_target="tpu_custom_call" | custom-call | tf_op jit(solution)/shard_map/pallas_call | solution.py:318
  42.3 1.3 %copy.8 = f32[16,2,64,256]{3,2,1,0:T(8,128)} copy(f32[16,2,64,256]{3,2,1,0:T(8,128)S(1)} %shard_map.64) | data formatting | bytes 4194304
  (2 shorter events, 0.0 us)
Async XLA Ops:
  2.7 1.3 %copy-start = (f32[80,16,256]{2,1,0:T(8,128)S(1)}, f32[80,16,256]{2,1,0:T(8,128)}, u32[]{:S(2)}) copy-start(f32[80,16,256]{2,1,0:T(8,128)} %param.6) | copy-start | bytes 3932164
